TPU v7x, 256 devices: a whole 4x4x8 slice. The times are simulated.
256 devices in a mesh: shot: 16 (over y, x_lo, core), seq: 16 (over z, x_hi).
Axes of the slice: x: 4 (x_hi: 2, x_lo: 2; x = x_hi * 2 + x_lo), y: 4, z: 8, core: 2. Of those that a mesh axis runs over, the one named last changes fastest.
Arguments:
- query_rows: bfloat16 [16, 2048, 1536], P('shot', 'seq'), may hold values from -4.5188047 to 4.5188047
- key_rows: bfloat16 [16, 2048, 1536], P('shot', 'seq'), may hold values from -4.5188047 to 4.5188047
- value_rows: bfloat16 [16, 2048, 1536], P('shot', 'seq'), may hold values from -6 to 6
- out_grad: bfloat16 [16, 2048, 1536], P('shot', 'seq'), may hold values from -6 to 6
- shot_lengths: int32 [16], replicated, may hold values from 1024 to 2048, as said below
- global_positions: int32 [16, 16], P('shot'), may hold values from 0 to 2047, as said below
Outputs:
- attended: bfloat16 [16, 2048, 1536], P('shot', 'seq')
- query_grad: bfloat16 [16, 2048, 1536], P('shot', 'seq')
- key_grad: bfloat16 [16, 2048, 1536], P('shot', 'seq')
- value_grad: bfloat16 [16, 2048, 1536], P('shot', 'seq')
Inputs may be any that keep to these rules, and one draw needn't show every extreme that they name: `shot_lengths`: in every draw one shot has 2048 tokens and another 2048 // 2. `global_positions`: in each shot, entries 1 * b to 1 * (b + 1) - 1 are distinct positions among rows 128 * b to 128 * (b + 1) - 1, for every b.
All inputs are finite; a program needn't handle non-finite values.
Results may differ from a plain program's by a relative error of at most 0.023.
Values may be sent and summed in bfloat16 or wider, within the bound.
A program may use at most 128 MiB of HBM per device.

v0:
```python
import math

import jax
import jax.numpy as jnp
from jax import lax
from jax.sharding import PartitionSpec as P

HEADS = 12
HEAD_DIM = 128


NEG_FILL = -1e30


def masked_logits(query_heads, key_block, usable, score_scale):
    logits = (
        jnp.einsum("ihd,jhd->hij", query_heads, key_block, preferred_element_type=jnp.float32)
        * score_scale
    )
    return jnp.where(usable[None, None, :], logits, NEG_FILL)


def body(query_rows, key_rows, value_rows, out_grad, shot_lengths, global_positions):
    row_count = query_rows.shape[1]
    features = query_rows.shape[2]
    seq_count = lax.axis_size("seq")
    shot_count = lax.axis_size("shot")
    shot_index = lax.axis_index("shot")
    seq_index = lax.axis_index("seq")
    glob_count = global_positions.shape[1] // seq_count
    score_scale = 1.0 / math.sqrt(HEAD_DIM)
    own_queries = query_rows[0]
    own_keys = key_rows[0]
    own_values = value_rows[0]
    own_grads = out_grad[0]
    length = lax.dynamic_index_in_dim(shot_lengths, shot_index, 0, keepdims=False)
    shot_positions = global_positions[0]
    positions = jnp.arange(row_count * seq_count, dtype=jnp.int32)
    is_global = jnp.any(positions[:, None] == shot_positions[None, :], axis=1)
    alive_mask = (positions < length) | is_global
    local_alive = lax.dynamic_slice_in_dim(alive_mask, seq_index * row_count, row_count, 0)
    own_positions = (
        lax.dynamic_slice_in_dim(shot_positions, seq_index * glob_count, glob_count, 0)
        - seq_index * row_count
    )
    glob_keys = jnp.take(own_keys, own_positions, axis=0)
    glob_values = jnp.take(own_values, own_positions, axis=0)
    shot_keys, shot_values = (
        lax.all_gather(own_keys, "seq", axis=0, tiled=True),
        lax.all_gather(own_values, "seq", axis=0, tiled=True),
    )
    cross_keys, cross_values = (
        lax.all_gather(glob_keys, ("shot", "seq"), axis=0, tiled=True),
        lax.all_gather(glob_values, ("shot", "seq"), axis=0, tiled=True),
    )
    cross_owner = jnp.arange(shot_count * seq_count * glob_count, dtype=jnp.int32) // (
        seq_count * glob_count
    )
    cross_alive = cross_owner != shot_index
    query_heads = own_queries.reshape(row_count, HEADS, HEAD_DIM)
    grad_heads = own_grads.reshape(row_count, HEADS, HEAD_DIM)
    shot_key_heads = shot_keys.reshape(-1, HEADS, HEAD_DIM)
    shot_value_heads = shot_values.reshape(-1, HEADS, HEAD_DIM)
    cross_key_heads = cross_keys.reshape(-1, HEADS, HEAD_DIM)
    cross_value_heads = cross_values.reshape(-1, HEADS, HEAD_DIM)
    shot_logits = masked_logits(query_heads, shot_key_heads, alive_mask, score_scale)
    cross_logits = masked_logits(query_heads, cross_key_heads, cross_alive, score_scale)
    row_max = jnp.maximum(jnp.max(shot_logits, axis=-1), jnp.max(cross_logits, axis=-1))
    totals = jnp.sum(
        jnp.where(alive_mask[None, None, :], jnp.exp(shot_logits - row_max[..., None]), 0.0),
        axis=-1,
    )
    totals = totals + jnp.sum(
        jnp.where(cross_alive[None, None, :], jnp.exp(cross_logits - row_max[..., None]), 0.0),
        axis=-1,
    )
    row_lse = row_max + jnp.log(totals)
    shot_weights = jnp.where(
        alive_mask[None, None, :], jnp.exp(shot_logits - row_lse[..., None]), 0.0
    )
    cross_weights = jnp.where(
        cross_alive[None, None, :], jnp.exp(cross_logits - row_lse[..., None]), 0.0
    )
    shot_low = shot_weights.astype(jnp.bfloat16)
    cross_low = cross_weights.astype(jnp.bfloat16)
    output_heads = jnp.einsum(
        "hij,jhd->ihd", shot_low, shot_value_heads, preferred_element_type=jnp.float32
    )
    output_heads = output_heads + jnp.einsum(
        "hij,jhd->ihd", cross_low, cross_value_heads, preferred_element_type=jnp.float32
    )
    attended = output_heads.astype(jnp.bfloat16)
    delta = jnp.sum(grad_heads.astype(jnp.float32) * attended.astype(jnp.float32), axis=-1)
    shot_dprod = jnp.einsum(
        "ihd,jhd->hij", grad_heads, shot_value_heads, preferred_element_type=jnp.float32
    )
    cross_dprod = jnp.einsum(
        "ihd,jhd->hij", grad_heads, cross_value_heads, preferred_element_type=jnp.float32
    )
    shot_dlogits = (shot_weights * (shot_dprod - delta.T[..., None])).astype(jnp.bfloat16)
    cross_dlogits = (cross_weights * (cross_dprod - delta.T[..., None])).astype(jnp.bfloat16)
    query_sum = jnp.einsum(
        "hij,jhd->ihd", shot_dlogits, shot_key_heads, preferred_element_type=jnp.float32
    )
    query_sum = query_sum + jnp.einsum(
        "hij,jhd->ihd", cross_dlogits, cross_key_heads, preferred_element_type=jnp.float32
    )
    query_grad = (score_scale * query_sum).astype(jnp.bfloat16)
    cross_key_part = score_scale * jnp.einsum(
        "hij,ihd->jhd", cross_dlogits, query_heads, preferred_element_type=jnp.float32
    )
    cross_value_part = jnp.einsum(
        "hij,ihd->jhd", cross_low, grad_heads, preferred_element_type=jnp.float32
    )
    cross_key_part = cross_key_part.reshape(-1, features)
    cross_value_part = cross_value_part.reshape(-1, features)
    all_lse, all_delta = (
        lax.all_gather(row_lse.T, "seq", axis=0, tiled=True),
        lax.all_gather(delta, "seq", axis=0, tiled=True),
    )
    local_key_heads = own_keys.reshape(row_count, HEADS, HEAD_DIM)
    local_value_heads = own_values.reshape(row_count, HEADS, HEAD_DIM)

    def key_block(carry, pieces, start):
        piece_queries, piece_grads = pieces
        piece_rows = piece_queries.shape[0]
        piece_query_heads = piece_queries.reshape(piece_rows, HEADS, HEAD_DIM)
        piece_grad_heads = piece_grads.reshape(piece_rows, HEADS, HEAD_DIM)
        logits = (
            jnp.einsum(
                "ihd,jhd->hij",
                piece_query_heads,
                local_key_heads,
                preferred_element_type=jnp.float32,
            )
            * score_scale
        )
        weights = jnp.where(local_alive[None, None, :], jnp.exp(logits - all_lse.T[..., None]), 0.0)
        dprod = jnp.einsum(
            "ihd,jhd->hij", piece_grad_heads, local_value_heads, preferred_element_type=jnp.float32
        )
        dlogits = (weights * (dprod - all_delta.T[..., None])).astype(jnp.bfloat16)
        key_total = jnp.einsum(
            "hij,ihd->jhd", dlogits, piece_query_heads, preferred_element_type=jnp.float32
        )
        value_total = jnp.einsum(
            "hij,ihd->jhd",
            weights.astype(jnp.bfloat16),
            piece_grad_heads,
            preferred_element_type=jnp.float32,
        )
        return (key_total, value_total)

    zero_block = jnp.zeros((row_count, HEADS, HEAD_DIM), jnp.float32)
    key_total, value_total = key_block(
        (zero_block, zero_block),
        (
            lax.all_gather(own_queries, "seq", axis=0, tiled=True),
            lax.all_gather(own_grads, "seq", axis=0, tiled=True),
        ),
        jnp.int32(0),
    )
    key_received, value_received = (
        lax.psum_scatter(cross_key_part, ("shot", "seq"), scatter_dimension=0, tiled=True),
        lax.psum_scatter(cross_value_part, ("shot", "seq"), scatter_dimension=0, tiled=True),
    )
    onehot_rows = (
        jnp.arange(row_count, dtype=jnp.int32)[:, None] == own_positions[None, :]
    ).astype(jnp.float32)
    key_grad = score_scale * key_total.reshape(row_count, features)
    key_grad = key_grad + jnp.dot(onehot_rows, key_received, precision=lax.Precision.HIGHEST)
    value_grad = value_total.reshape(row_count, features)
    value_grad = value_grad + jnp.dot(onehot_rows, value_received, precision=lax.Precision.HIGHEST)
    return (
        attended.reshape(1, row_count, features),
        query_grad.reshape(1, row_count, features),
        key_grad.astype(jnp.bfloat16).reshape(1, row_count, features),
        value_grad.astype(jnp.bfloat16).reshape(1, row_count, features),
    )


def solution(mesh):
    placed = (
        P("shot", "seq", None),
        P("shot", "seq", None),
        P("shot", "seq", None),
        P("shot", "seq", None),
        P(),
        P("shot", None),
    )
    return jax.shard_map(
        body,
        mesh=mesh,
        in_specs=placed,
        out_specs=(
            P("shot", "seq", None),
            P("shot", "seq", None),
            P("shot", "seq", None),
            P("shot", "seq", None),
        ),
        check_vma=False,
    )
```

profile of v0, /device:TPU:1, one launch (start us, length us, event | category | flops | bytes accessed | tf_op | source)
XLA Modules:
  0.0 1732.3 jit_solution(16886195066031517965)
XLA Ops:
  7.2 1.9 copy.158
  10.0 1.9 copy.157
  12.0 2.0 copy.167
  14.0 1.9 copy.178
  15.9 1.2 constant_dynamic-slice_fusion
  18.6 623.0 %all-gather.4 = bf16[256,1,1536]{2,1,0:T(2,128)(2,1)S(1)} all-gather(bf16[1,1,1536]{2,1,0:T(2,128)(2,1)S(1)} %fusion.41), channel_id=1, replica_groups=mesh['shot'=16,'seq'=16] {'shot','seq'}, dimensions={0}, use_global_device_ids=true | all-gather | bytes 789504 | tf_op jit(solution)/shard_map/all_gather | solution.py:53
  641.6 1.3 copy.161
  643.7 627.5 %all-gather.5 = bf16[256,1,1536]{2,1,0:T(2,128)(2,1)S(1)} all-gather(bf16[1,1,1536]{2,1,0:T(2,128)(2,1)S(1)} %fusion.42), channel_id=1, replica_groups=mesh['shot'=16,'seq'=16] {'shot','seq'}, dimensions={0}, use_global_device_ids=true | all-gather | bytes 789504 | tf_op jit(solution)/shard_map/all_gather | solution.py:54
  1271.2 2.8 copy.165
  1277.1 9.7 fusion.2
  1286.8 8.8 copy.164
  1295.9 6.6 select_reduce_fusion
  1302.5 9.9 fusion.26
  1313.0 0.9 copy.188
  1313.9 2.6 fusion.20
  1316.5 13.3 fusion.32
  1329.8 2.6 fusion.35
  1332.4 1.9 copy.189
  1334.3 34.3 %all_gather.31 = f32[2048,12]{0,1:T(8,128)} all-gather(f32[128,12]{0,1:T(8,128)S(1)} %get-tuple-element.48), channel_id=1, replica_groups=mesh['shot'=16,'seq'=16] {'seq'}, dimensions={0}, use_global_device_ids=true | all-gather | bytes 104448 | tf_op jit(solution)/shard_map/all_gather | solution.py:119
  1368.6 32.1 %all_gather.29 = f32[2048,12]{0,1:T(8,128)} all-gather(f32[128,12]{0,1:T(8,128)S(1)} %bitcast.144), channel_id=1, replica_groups=mesh['shot'=16,'seq'=16] {'seq'}, dimensions={0}, use_global_device_ids=true | all-gather | bytes 104448 | tf_op jit(solution)/shard_map/all_gather | solution.py:118
  1400.6 2.7 multiply_bitcast_fusion
  1403.3 2.3 fusion.55
  1405.6 9.3 fusion.58
  1415.0 9.8 fusion.3
  1424.8 2.3 copy.187
  1427.1 1.7 copy.183
  1428.8 1.6 copy.186
  1430.5 13.1 fusion.34
  1443.8 278.3 %all-reduce.5.cloned.1.call-done = (f32[256,1536]{0,1:T(8,128)}, f32[256,1536]{1,0:T(8,128)}) async-done(((f32[256,1536]{0,1:T(8,128)}, f32[256,1536]{1,0:T(8,128)}), (f32[256,1536]{0,1:T(8,128)}, f32[256,1536]{1,0:T(8,128)})) %all-reduce.5.cloned.1.call-update) | async-done | bytes 3145744
  1722.2 0.8 dynamic-slice_reduce_fusion.1
  1723.0 1.6 dynamic-slice_reduce_fusion
  1724.7 1.1 fusion.38
  (64 shorter events, 6.7 us)
Async XLA Ops:
  7.2 1267.5 %copy-start.14 = (s32[1,16]{1,0:T(1,128)S(1)}, s32[1,16]{1,0:T(1,128)}, u32[]{:S(2)}) copy-start(s32[1,16]{1,0:T(1,128)} %param.13) | copy-start | bytes 196
  7.2 1266.9 %copy-start.16 = (s32[16]{0:T(128)S(1)}, s32[16]{0:T(128)}, u32[]{:S(2)}) copy-start(s32[16]{0:T(128)} %param.12) | copy-start | bytes 196
  7.2 1269.9 %all-gather.11.cloned.1.call-start = ((), (), s32[]{:S(2)}) async-start(), calls=%async_computation | async-start | bytes 6684672 | tf_op jit(solution)/shard_map/all_gather | solution.py:49
  9.2 1277.6 %all-gather.13.cloned.1.call-start = ((), (), s32[]{:S(2)}) async-start(), calls=%async_computation.1 | async-start | bytes 6684672 | tf_op jit(solution)/shard_map/all_gather | solution.py:50
  9.9 1395.7 %all-gather.15.cloned.1.call-start = ((), (), s32[]{:S(2)}) async-start(), calls=%async_computation.2 | async-start | bytes 6684672 | tf_op jit(solution)/shard_map/all_gather | solution.py:158
  11.9 1264.7 %copy-start = (bf16[1,128,1536]{1,2,0:T(8,128)(2,1)S(1)}, bf16[1,128,1536]{1,2,0:T(8,128)(2,1)}, u32[]{:S(2)}) copy-start(bf16[1,128,1536]{1,2,0:T(8,128)(2,1)} %copy.157) | copy-start | bytes 1179652
  11.9 1403.0 %all-gather.17.cloned.1.call-start = ((), (), s32[]{:S(2)}) async-start(), calls=%async_computation.3 | async-start | bytes 6684672 | tf_op jit(solution)/shard_map/all_gather | solution.py:159
  14.0 1708.2 %all-reduce.5.cloned.1.call-start = ((), (), s32[]{:S(2)}) async-start(), calls=%async_computation.4 | async-start | bytes 6291456
  1275.4 27.1 %copy-start.11 = (pred[2048]{0:T(1024)(128)(4,1)}, pred[2048]{0:T(1024)(128)(4,1)S(1)}, u32[]{:S(2)}) copy-start(pred[2048]{0:T(1024)(128)(4,1)S(1)} %fusion.40) | copy-start | bytes 6148
  1276.0 19.5 %copy-start.12 = (pred[256]{0:T(512)(128)(4,1)}, pred[256]{0:T(512)(128)(4,1)S(1)}, u32[]{:S(2)}) copy-start(pred[256]{0:T(512)(128)(4,1)S(1)} %fusion.43) | copy-start | bytes 772
  1302.5 9.9 copy-start.1
  1302.5 9.9 copy-start.2
  1302.5 9.9 copy-start.13
  1329.8 75.8 %copy-start.5 = (bf16[1,128,1536]{1,2,0:T(8,128)(2,1)S(1)}, bf16[1,128,1536]{1,2,0:T(8,128)(2,1)}, u32[]{:S(2)}) copy-start(bf16[1,128,1536]{1,2,0:T(8,128)(2,1)} %copy.158) | copy-start | bytes 1179652
  1405.6 9.3 copy-start.9
  1405.6 9.3 copy-start.17
  1414.9 12.2 copy-start.3
  1414.9 13.9 copy-start.4
  1424.8 5.7 copy-start.7
  1428.8 1.7 copy-start.8
  1428.8 1.7 copy-start.10
  1430.5 294.2 %copy-start.6 = (f32[128,1536]{1,0:T(8,128)S(1)}, f32[128,1536]{1,0:T(8,128)}, u32[]{:S(2)}) copy-start(f32[128,1536]{1,0:T(8,128)} %copy.187) | copy-start | bytes 2359300
  1430.5 294.2 %copy-start.15 = (f32[128]{0:T(128)S(1)}, f32[128]{0:T(128)}, u32[]{:S(2)}) copy-start(f32[128]{0:T(128)} %fusion.44) | copy-start | bytes 1540
Sparse Core Ops, SparseCore 0:
  10.5 131.6 all-gather.10
  144.8 114.8 all-gather.12
  262.8 124.2 all-gather.14
  389.9 124.9 all-gather.16
  1430.6 291.5 all-reduce.4
where the time goes:
time: 1730 us
  blocking collectives  1320 us (76%)
  waiting for transfers between devices  279 us (16%)
  matrix products  76.2 us (4%)
  local copies, waits for them, and re-layouts  34.4 us (2%)
    all_gather x1, blocking collectives, body(): lax.all_gather(glob_values, ('shot', 'seq'), axis=0, tiled=True)  628 us
    all_gather x1, blocking collectives, body(): lax.all_gather(glob_keys, ('shot', 'seq'), axis=0, tiled=True)  623 us
    unnamed x6, waiting for transfers between devices  279 us
  transfers between devices with their start and end apart: 5, of which 1 were waited for; matrix products, arithmetic and copies ran while one was open for 6% of the time, Pallas kernels for 0%

commit v1 on v0

v1 whole, which is shorter than its diff:
```python
import math

import jax
import jax.numpy as jnp
from jax import lax
from jax.experimental import pallas as pl
from jax.experimental.pallas import tpu as pltpu
from jax.sharding import PartitionSpec as P

MESH = pl.DeviceIdType.MESH
F32, BF16, I32 = jnp.float32, jnp.bfloat16, jnp.int32
HEADS, D = 12, 128
SEQ, SHOTS = 16, 16
ROWS = 128
OWN = SEQ * ROWS
CROSS = SHOTS * SEQ
KEYS = OWN + CROSS
QB = 256
KC = 768
SCALE = 1.0 / math.sqrt(D)
LOGIT2 = SCALE * math.log2(math.e)
MASKED = -1e30


def nt(a, b):
    return lax.dot_general(a, b, (((1,), (1,)), ((), ())), preferred_element_type=F32)


def nn(a, b):
    return jnp.dot(a, b, preferred_element_type=F32)


def zstep(i):
    return ((i + 1) // 2) * (2 * (i % 2) - 1)


def owns(t):
    r = t % 8
    return jnp.logical_or(r == 0, r % 3 != 0)


def head_of(t):
    r = t % 8
    return 6 * (t // 8) + r - (r + 4) // 8 - (r + 1) // 8


def at128(i):
    return pl.ds(pl.multiple_of(i * 128, 128), 128)


def at256(i):
    return pl.ds(pl.multiple_of(i * 256, 256), 256)


def attend(i, kx, vx, kb, qx, gx, kt, vt, logit, prob, dlog, gn, ox, dqx):
    rows = at256(i)
    q = qx[rows, :]
    g = gx[rows, :]
    qa = jnp.concatenate([q, jnp.ones((QB, D), BF16)], 1)
    top = None
    for c in range(KEYS // KC):
        ks = slice(c * KC, (c + 1) * KC)
        s = nt(jnp.concatenate([kx[ks, :], kb[ks, :]], 1), qa)
        logit[ks, :] = s
        m = jnp.max(s.reshape(KC // 8, 8, QB), axis=0)
        top = m if top is None else jnp.maximum(top, m)
    top = jnp.max(top, axis=0, keepdims=True) * LOGIT2
    acc = None
    for c in range(KEYS // KC):
        ks = slice(c * KC, (c + 1) * KC)
        p = jnp.exp2(logit[ks, :] * LOGIT2 - top).astype(BF16)
        prob[ks, rows] = p
        part = nn(vt[:, ks], p)
        acc = part if acc is None else acc + part
    total = jnp.broadcast_to(acc[128:129, :], (D, QB))
    both = jnp.concatenate([acc[:128], total], 0).T
    inv = 1.0 / both[:, 128:]
    att = (both[:, :128] * inv).astype(BF16)
    ox[rows, :] = att
    gf = g.astype(F32)
    delta = jnp.sum(gf * att.astype(F32), axis=1, keepdims=True) * inv
    gs = (gf * inv).astype(BF16)
    gn[rows, :] = gs
    high = delta.astype(BF16).astype(F32)
    lane = lax.broadcasted_iota(I32, (QB, D), 1)
    tail = jnp.where(lane == 0, high, jnp.where(lane == 1, delta - high, 0.0))
    ga = jnp.concatenate([gs, tail.astype(BF16)], 1)
    lane = lax.broadcasted_iota(I32, (KC, D), 1)
    minus = jnp.where(lane < 2, -1.0, 0.0).astype(BF16)
    acc = None
    for c in range(KEYS // KC):
        ks = slice(c * KC, (c + 1) * KC)
        dp = nt(jnp.concatenate([vx[ks, :], minus], 1), ga)
        ds = prob[ks, rows] * dp.astype(BF16)
        dlog[ks, rows] = ds
        part = nn(kt[:, ks], ds)
        acc = part if acc is None else acc + part
    dqx[rows, :] = (acc * SCALE).T.astype(BF16)


def kernel(
    lens, pos, q, k, v, g, o, dq, dk, dv,
    kx, vx, kb, qx, gx, kt, vt, logit, prob, dlog, gn, ox, dqx, dkx, dvx,
    xs, xg, xr, xc, xl, lk, lv,
    in_send, kv_recv, q_recv, g_recv, in_own, x_send, x_recv, out_send, out_recv, out_own, c_send, c_recv,
):
    me, sh = lax.axis_index("seq"), lax.axis_index("shot")
    z, x = me // 2, me % 2
    mine = owns(me)
    head = head_of(me)

    barrier = pltpu.get_barrier_semaphore()

    def greet(j, _):
        pl.semaphore_signal(barrier, inc=1, device_id=(sh, (me + j) % SEQ), device_id_type=MESH)
        pl.semaphore_signal(barrier, inc=1, device_id=((sh + j) % SHOTS, me), device_id_type=MESH)
        return 0

    lax.fori_loop(1, 16, greet, 0)
    pl.semaphore_wait(barrier, 30)

    def remote(src, dst, send, recv, to):
        return pltpu.make_async_remote_copy(
            src_ref=src, dst_ref=dst, send_sem=send, recv_sem=recv, device_id=to, device_id_type=MESH
        )

    def partner(j):
        return 2 * ((z - zstep(j // 2) + 8) % 8) + (x + j) % 2

    def send_kv(j, _):
        t = partner(j)

        @pl.when(owns(t))
        def _():
            cols = at128(head_of(t))
            remote(k.at[0, :, cols], kx.at[at128(me), :], in_send.at[0], kv_recv.at[0], (sh, t)).start()
            remote(v.at[0, :, cols], vx.at[at128(me), :], in_send.at[1], kv_recv.at[1], (sh, t)).start()

        return 0

    def send_qg(j, _):
        t = partner(j)
        i = j // 2

        @pl.when(owns(t))
        def _():
            cols = at128(head_of(t))
            slot = at128(2 * i + x)
            remote(q.at[0, :, cols], qx.at[slot, :], in_send.at[2], q_recv.at[i], (sh, t)).start()
            remote(g.at[0, :, cols], gx.at[slot, :], in_send.at[3], g_recv.at[i], (sh, t)).start()

        return 0

    def own_in():
        cols = at128(head)
        return (
            pltpu.make_async_copy(k.at[0, :, cols], kx.at[at128(me), :], in_own.at[0]),
            pltpu.make_async_copy(v.at[0, :, cols], vx.at[at128(me), :], in_own.at[1]),
            pltpu.make_async_copy(q.at[0, :, cols], qx.at[at128(x), :], in_own.at[2]),
            pltpu.make_async_copy(g.at[0, :, cols], gx.at[at128(x), :], in_own.at[3]),
        )

    def own_out():
        cols = at128(head)
        return (
            pltpu.make_async_copy(ox.at[at128(x), :], o.at[0, :, cols], out_own.at[0]),
            pltpu.make_async_copy(dqx.at[at128(x), :], dq.at[0, :, cols], out_own.at[1]),
            pltpu.make_async_copy(dkx.at[at128(me), :], lk.at[:, cols], out_own.at[2]),
            pltpu.make_async_copy(dvx.at[at128(me), :], lv.at[:, cols], out_own.at[3]),
        )

    @pl.when(mine)
    def _():
        for copy in own_in():
            copy.start()

    lax.fori_loop(1, SEQ, send_kv, 0)
    lax.fori_loop(1, SEQ, send_qg, 0)

    @pl.when(mine)
    def _():
        length = lens[sh]
        here = (sh, me)
        row = lax.broadcasted_iota(I32, (ROWS, D), 0)
        lane = lax.broadcasted_iota(I32, (ROWS, D), 1)
        for b in range(SEQ):
            alive = jnp.logical_or(row + b * ROWS < length, row + b * ROWS == pos[0, b])
            dead = jnp.logical_and(jnp.logical_not(alive), lane == 0)
            kb[b * ROWS : (b + 1) * ROWS, :] = jnp.where(dead, MASKED, 0.0).astype(BF16)
        for b in range(CROSS // ROWS):
            dead = jnp.logical_and((row + b * ROWS) // SEQ == sh, lane == 0)
            kb[OWN + b * ROWS : OWN + (b + 1) * ROWS, :] = jnp.where(dead, MASKED, 0.0).astype(BF16)
        vt[D : D + 16, :] = jnp.ones((16, KEYS), BF16)
        sub = lax.broadcasted_iota(I32, (SEQ, OWN), 0)
        at = jnp.full((SEQ, OWN), -1, I32)
        for b in range(SEQ):
            at = jnp.where(sub == b, pos[0, b], at)
        pick = jnp.where(lax.broadcasted_iota(I32, (SEQ, OWN), 1) == at, 1.0, 0.0).astype(BF16)

        for n, (buf, copy) in enumerate(zip((kx, vx), own_in())):
            part = buf.at[pl.ds(0, OWN - ROWS), :]
            remote(part, part, in_send.at[n], kv_recv.at[n], here).wait_recv()
            copy.wait()
            rows = nn(pick, buf[0:OWN, :]).astype(BF16)
            xs[n] = rows
            buf[pl.ds(pl.multiple_of(OWN + sh * SEQ, SEQ), SEQ), :] = rows

        def send_x(j, _):
            to = ((sh + j) % SHOTS, me)
            dst = pl.ds(pl.multiple_of(OWN + sh * SEQ, SEQ), SEQ)
            remote(xs.at[0], kx.at[dst, :], x_send.at[0], x_recv.at[0], to).start()
            remote(xs.at[1], vx.at[dst, :], x_send.at[1], x_recv.at[1], to).start()
            return 0

        lax.fori_loop(1, SHOTS, send_x, 0)

        def turn(c, _):
            kt[:, at256(c)] = kx[at256(c), :].T
            vt[0:D, at256(c)] = vx[at256(c), :].T
            return 0

        lax.fori_loop(0, OWN // 256, turn, 0)
        for n, buf in enumerate((kx, vx)):
            part = buf.at[pl.ds(OWN, CROSS - SEQ), :]
            remote(part, part, x_send.at[n], x_recv.at[n], here).wait()
        lax.fori_loop(OWN // 256, KEYS // 256, turn, 0)

        def step(i, _):
            for n, (buf, sem) in enumerate(((qx, q_recv), (gx, g_recv))):

                @pl.when(i == 0)
                def _(n=n, buf=buf, sem=sem):
                    part = buf.at[at128(1 - x), :]
                    remote(part, part, in_send.at[2 + n], sem.at[i], here).wait_recv()
                    own_in()[2 + n].wait()

                @pl.when(i > 0)
                def _(n=n, buf=buf, sem=sem):
                    part = buf.at[at256(i), :]
                    remote(part, part, in_send.at[2 + n], sem.at[i], here).wait_recv()

            attend(i, kx, vx, kb, qx, gx, kt, vt, logit, prob, dlog, gn, ox, dqx)
            cols = at128(head)
            for d in range(2):
                xt = (x + d) % 2
                to = (sh, 2 * ((z + zstep(i) + 8) % 8) + xt)
                slot = at128(2 * i + xt)

                def start(slot=slot, to=to):
                    remote(ox.at[slot, :], o.at[0, :, cols], out_send.at[0], out_recv.at[0], to).start()
                    remote(dqx.at[slot, :], dq.at[0, :, cols], out_send.at[1], out_recv.at[1], to).start()

                if d == 1:
                    start()
                else:
                    pl.when(i > 0)(start)

                    @pl.when(i == 0)
                    def _():
                        own_out()[0].start()
                        own_out()[1].start()

            return 0

        lax.fori_loop(0, SEQ // 2, step, 0)

        cross = pl.ds(OWN, CROSS)
        xg[:, 0:SEQ, :] = (nn(dlog[cross, :], qx[...]) * SCALE).reshape(SHOTS, SEQ, D)
        xg[:, SEQ : 2 * SEQ, :] = nn(prob[cross, :], gn[...]).reshape(SHOTS, SEQ, D)
        xr[pl.ds(sh, 1)] = jnp.zeros((1, 2 * SEQ, D), F32)

        def send_g(j, _):
            s = (sh + j) % SHOTS
            remote(xg.at[s], xr.at[sh], x_send.at[2], x_recv.at[2], (s, me)).start()
            return 0

        lax.fori_loop(1, SHOTS, send_g, 0)

        def finish(i, _):
            zt = (z + zstep(i) + 8) % 8
            rows = at256(zt)
            cols = at128(head)
            dkx[rows, :] = (nn(dlog[rows, :], qx[...]) * SCALE).astype(BF16)
            dvx[rows, :] = nn(prob[rows, :], gn[...]).astype(BF16)
            for d in range(2):
                t = 2 * zt + (x + d) % 2

                def start(t=t):
                    remote(dkx.at[at128(t), :], lk.at[:, cols], out_send.at[2], out_recv.at[2], (sh, t)).start()
                    remote(dvx.at[at128(t), :], lv.at[:, cols], out_send.at[3], out_recv.at[3], (sh, t)).start()

                if d == 1:
                    start()
                else:
                    pl.when(i > 0)(start)

                    @pl.when(i == 0)
                    def _():
                        own_out()[2].start()
                        own_out()[3].start()

            return 0

        lax.fori_loop(0, SEQ // 2, finish, 0)

        part = xr.at[pl.ds(0, SHOTS - 1)]
        remote(part, part, x_send.at[2], x_recv.at[2], here).wait()
        total = jnp.sum(xr[...], axis=0)
        xc[...] = jnp.zeros_like(xc)
        for b in range(SEQ):
            xc[b, 0:1, :] = total[b : b + 1, :]
            xc[b, 1:2, :] = total[SEQ + b : SEQ + b + 1, :]
        xl[pl.ds(head, 1)] = xc[pl.ds(me, 1)]

        def send_c(j, _):
            t = (me + j) % SEQ
            remote(xc.at[t], xl.at[head], c_send, c_recv, (sh, t)).start()
            return 0

        lax.fori_loop(1, SEQ, send_c, 0)

        for n, buf in enumerate((ox, dqx, dkx, dvx)):
            part = buf.at[pl.ds(0, OWN - ROWS), :]
            remote(part, part, out_send.at[n], out_recv.at[n], here).wait_send()
            own_out()[n].wait()
        part = xc.at[pl.ds(0, SEQ - 1)]
        remote(part, part, c_send, c_recv, here).wait_send()

    def settle(count):
        here = (sh, me)
        for n, buf in enumerate((k, v, q, g)):
            part = buf.at[0, :, pl.ds(0, count * D)]
            remote(part, part, in_send.at[n], out_recv.at[n], here).wait_send()
        for n, buf in enumerate((o.at[0], dq.at[0], lk, lv)):
            part = buf.at[:, pl.ds(0, count * D)]
            remote(part, part, out_send.at[n], out_recv.at[n], here).wait_recv()
        part = xl.at[pl.ds(0, count)]
        remote(part, part, c_send, c_recv, here).wait_recv()

    @pl.when(mine)
    def _():
        settle(HEADS - 1)

    @pl.when(jnp.logical_not(mine))
    def _():
        settle(HEADS)

    there = lax.broadcasted_iota(I32, (ROWS, D), 0) == pos[0, me] - me * ROWS
    for h in range(HEADS):
        cols = slice(h * D, (h + 1) * D)
        add = xl[h]
        dk[0, :, cols] = (lk[:, cols].astype(F32) + jnp.where(there, add[0:1, :], 0.0)).astype(BF16)
        dv[0, :, cols] = (lv[:, cols].astype(F32) + jnp.where(there, add[1:2, :], 0.0)).astype(BF16)


def body(query_rows, key_rows, value_rows, out_grad, shot_lengths, global_positions):
    smem = pl.BlockSpec(memory_space=pltpu.SMEM)
    hbm = pl.BlockSpec(memory_space=pl.ANY)
    vmem = pl.BlockSpec(memory_space=pltpu.VMEM)
    shape = jax.ShapeDtypeStruct(query_rows.shape, BF16)
    dma = pltpu.SemaphoreType.DMA
    return tuple(
        pl.pallas_call(
            kernel,
            out_shape=(shape,) * 4,
            in_specs=[smem, smem, hbm, hbm, hbm, hbm],
            out_specs=(hbm, hbm, vmem, vmem),
            scratch_shapes=[
                pltpu.VMEM((KEYS, D), BF16),
                pltpu.VMEM((KEYS, D), BF16),
                pltpu.VMEM((KEYS, D), BF16),
                pltpu.VMEM((OWN, D), BF16),
                pltpu.VMEM((OWN, D), BF16),
                pltpu.VMEM((D, KEYS), BF16),
                pltpu.VMEM((D + 16, KEYS), BF16),
                pltpu.VMEM((KEYS, QB), F32),
                pltpu.VMEM((KEYS, OWN), BF16),
                pltpu.VMEM((KEYS, OWN), BF16),
                pltpu.VMEM((OWN, D), BF16),
                pltpu.VMEM((OWN, D), BF16),
                pltpu.VMEM((OWN, D), BF16),
                pltpu.VMEM((OWN, D), BF16),
                pltpu.VMEM((OWN, D), BF16),
                pltpu.VMEM((2, SEQ, D), BF16),
                pltpu.VMEM((SHOTS, 2 * SEQ, D), F32),
                pltpu.VMEM((SHOTS, 2 * SEQ, D), F32),
                pltpu.VMEM((SEQ, 8, D), F32),
                pltpu.VMEM((HEADS, 8, D), F32),
                pltpu.VMEM((ROWS, HEADS * D), BF16),
                pltpu.VMEM((ROWS, HEADS * D), BF16),
                dma((4,)),
                dma((2,)),
                dma((SEQ // 2,)),
                dma((SEQ // 2,)),
                dma((4,)),
                dma((3,)),
                dma((3,)),
                dma((4,)),
                dma((4,)),
                dma((4,)),
                dma,
                dma,
            ],
            compiler_params=pltpu.CompilerParams(
                collective_id=0, has_side_effects=True, vmem_limit_bytes=48 << 20
            ),
        )(shot_lengths, global_positions, query_rows, key_rows, value_rows, out_grad)
    )


def solution(mesh):
    rows = P("shot", "seq", None)
    return jax.shard_map(
        body,
        mesh=mesh,
        in_specs=(rows, rows, rows, rows, P(), P("shot", None)),
        out_specs=(rows,) * 4,
        check_vma=False,
    )
```

time: 1730 us -> 118 us (0.07)
  blocking collectives: 1320 us -> 0 us
  waiting for transfers between devices: 279 us -> 0 us
  Pallas kernels: 0 us -> 109 us
  matrix products: 76.2 us -> 0 us
  local copies, waits for them, and re-layouts: 34.4 us -> 8.27 us
    all_gather x4 -> x0, blocking collectives: 1320 us -> none  [the longest x1 628 us: body(): lax.all_gather(glob_values, ('shot', 'seq'), axis=0, tiled=True)]
    unnamed x6 -> x0, waiting for transfers between devices: 279 us -> none
    pallas_call x0 -> x1, Pallas kernels: none -> 109 us  [body(): pl.pallas_call(kernel, out_shape=(shape,) * 4, in_specs=[smem, smem, hbm,...]
    dot_general x12 -> x0, matrix products: 76.2 us -> none  [the longest x1 13.3 us: body(): jnp.einsum('hij,jhd->ihd', shot_dlogits, shot_key_heads, preferred_elemen...]
  transfers between devices with their start and end apart: 5 -> 0, of which waited for: 1 -> 0; matrix products, arithmetic and copies ran while one was open for 6% -> 0% of each run, Pallas kernels for 0% -> 0%
where the time goes in v1:
time: 118 us
  Pallas kernels  109 us (92%)
  local copies, waits for them, and re-layouts  8.27 us (7%)
    pallas_call x1, Pallas kernels, body(): pl.pallas_call(kernel, out_shape=(shape,) * 4, in_specs=[smem, smem, hbm,...  109 us
    unnamed x16, local copies, waits for them, and re-layouts  8.27 us

profile of v1, /device:TPU:1, one launch (start us, length us, event | category | flops | bytes accessed | tf_op | source)
XLA Modules:
  0.0 118.0 jit_solution(15406991537506551665)
XLA Ops:
  0.6 0.0 copy-start
  0.6 1.0 copy-done
  1.6 0.0 copy-start.1
  1.6 1.0 copy-done.1
  2.6 0.0 copy-start.2
  2.6 1.0 copy-done.2
  3.6 0.0 copy-start.3
  3.6 1.0 copy-done.3
  4.6 0.0 copy-start.4
  4.6 0.7 copy-done.4
  5.3 0.0 copy-start.5
  5.3 0.7 copy-done.5
  5.9 109.1 %shard_map.93 = (bf16[1,128,1536]{2,1,0:T(8,128)(2,1)S(1)}, bf16[1,128,1536]{2,1,0:T(8,128)(2,1)S(1)}, bf16[1,128,1536]{2,1,0:T(8,128)(2,1)S(1)}, bf16[1,128,1536]{2,1,0:T(8,128)(2,1)S(1)}) custom-call(s32[16]{0:T(128)S(1)} %copy-done.4, s32[1,16]{1,0:T(1,128)S(1)} %copy-done.5, bf16[1,128,1536]{2,1,0:T(8,128)(2,1)S(1)} %copy-done, ...), custom_call_target="tpu_custom_call" | custom-call | tf_op jit(solution)/shard_map/pallas_call | solution.py:363
  115.0 0.7 copy.14
  115.8 0.7 copy.15
  116.5 0.7 copy.16
  117.3 0.7 copy.17
Async XLA Ops:
  0.6 1.0 copy-start
  1.6 1.0 copy-start.1
  2.6 1.0 copy-start.2
  3.6 1.0 copy-start.3
  4.6 0.7 copy-start.4
  5.3 0.7 copy-start.5

commit v2 on v1

v2 whole, which is shorter than its diff:
```python
import math

import jax
import jax.numpy as jnp
from jax import lax
from jax.experimental import pallas as pl
from jax.experimental.pallas import tpu as pltpu
from jax.sharding import PartitionSpec as P

MESH = pl.DeviceIdType.MESH
F32, BF16, I32 = jnp.float32, jnp.bfloat16, jnp.int32
HEADS, D = 12, 128
SEQ, SHOTS = 16, 16
ROWS = 128
OWN = SEQ * ROWS
CROSS = SHOTS * SEQ
KEYS = OWN + CROSS
QB = 256
KC = 768
SCALE = 1.0 / math.sqrt(D)
LOGIT2 = SCALE * math.log2(math.e)
MASKED = -1e30
EARLY = 5
CLOSE = 4
IDLE = ((0, 2, 5, 7), (8, 10, 13, 15))


def nt(a, b):
    return lax.dot_general(a, b, (((1,), (1,)), ((), ())), preferred_element_type=F32)


def nn(a, b):
    return jnp.dot(a, b, preferred_element_type=F32)


def zstep(i):
    return ((i + 1) // 2) * (2 * (i % 2) - 1)


def idle(shot):
    core = shot % 2
    return tuple(a + core * (b - a) for a, b in zip(*IDLE))


def owns(t, shot):
    found = t >= 0
    for s in idle(shot):
        found = jnp.logical_and(found, t != s)
    return found


def head_of(t, shot):
    return t - sum((t - s + 15) // 16 for s in idle(shot))


def owner_of(h, shot):
    return h + sum((h + n - s + 16) // 16 for n, s in enumerate(idle(shot)))


def at128(i):
    return pl.ds(pl.multiple_of(i * 128, 128), 128)


def at256(i):
    return pl.ds(pl.multiple_of(i * 256, 256), 256)


def attend(i, kx, vx, kb, qx, gx, kt, vt, logit, prob, dlog, gn, ox, dqx):
    rows = at256(i)
    q = qx[rows, :]
    g = gx[rows, :]
    qa = jnp.concatenate([q, jnp.ones((QB, D), BF16)], 1)
    top = None
    for c in range(KEYS // KC):
        ks = slice(c * KC, (c + 1) * KC)
        s = nt(jnp.concatenate([kx[ks, :], kb[ks, :]], 1), qa)
        logit[ks, :] = s
        m = jnp.max(s.reshape(KC // 8, 8, QB), axis=0)
        top = m if top is None else jnp.maximum(top, m)
    top = jnp.max(top, axis=0, keepdims=True) * LOGIT2
    acc = None
    for c in range(KEYS // KC):
        ks = slice(c * KC, (c + 1) * KC)
        p = jnp.exp2(logit[ks, :] * LOGIT2 - top).astype(BF16)
        prob[ks, rows] = p
        part = nn(vt[:, ks], p)
        acc = part if acc is None else acc + part
    total = jnp.broadcast_to(acc[128:129, :], (D, QB))
    both = jnp.concatenate([acc[:128], total], 0).T
    inv = 1.0 / both[:, 128:]
    att = (both[:, :128] * inv).astype(BF16)
    ox[rows, :] = att
    gf = g.astype(F32)
    delta = jnp.sum(gf * att.astype(F32), axis=1, keepdims=True) * inv
    gs = (gf * inv).astype(BF16)
    gn[rows, :] = gs
    high = delta.astype(BF16).astype(F32)
    lane = lax.broadcasted_iota(I32, (QB, D), 1)
    tail = jnp.where(lane == 0, high, jnp.where(lane == 1, delta - high, 0.0))
    ga = jnp.concatenate([gs, tail.astype(BF16)], 1)
    lane = lax.broadcasted_iota(I32, (KC, D), 1)
    minus = jnp.where(lane < 2, -1.0, 0.0).astype(BF16)
    acc = None
    for c in range(KEYS // KC):
        ks = slice(c * KC, (c + 1) * KC)
        dp = nt(jnp.concatenate([vx[ks, :], minus], 1), ga)
        ds = prob[ks, rows] * dp.astype(BF16)
        dlog[ks, rows] = ds
        part = nn(kt[:, ks], ds)
        acc = part if acc is None else acc + part
    dqx[rows, :] = (acc * SCALE).T.astype(BF16)


def kernel(
    lens_hbm, pos_hbm, q, k, v, g, o, dq, lk, lv, xl, lens, pos,
    kx, vx, kb, qx, gx, kt, vt, logit, prob, dlog, gn, ox, dqx, dkx, dvx,
    kin, vin, rowt, xin, xs, xg, xr, xc,
    in_send, kv_recv, q_recv, g_recv, in_own, x_send, x_recv, out_send, out_recv, out_own, c_send, c_recv, s_own, r_send, r_recv,
):
    me, sh = lax.axis_index("seq"), lax.axis_index("shot")
    z, x = me // 2, me % 2
    mine = owns(me, sh)
    head = head_of(me, sh)

    scalars = [
        pltpu.make_async_copy(lens_hbm, lens, s_own.at[0]),
        pltpu.make_async_copy(pos_hbm, pos, s_own.at[1]),
    ]
    whole = [
        pltpu.make_async_copy(k.at[0], kin, s_own.at[2]),
        pltpu.make_async_copy(v.at[0], vin, s_own.at[3]),
    ]
    for copy in scalars + whole:
        copy.start()
    barrier = pltpu.get_barrier_semaphore()

    def greet(j, _):
        pl.semaphore_signal(barrier, inc=1, device_id=(sh, (me + j) % SEQ), device_id_type=MESH)
        return 0

    def sibling(j):
        s = (sh + j) % SHOTS
        return (s, owner_of(head, s))

    def greet_sibling(j, _):
        pl.semaphore_signal(barrier, inc=1, device_id=sibling(j), device_id_type=MESH)
        return 0

    lax.fori_loop(1, SEQ, greet, 0)

    @pl.when(mine)
    def _():
        lax.fori_loop(1, SHOTS, greet_sibling, 0)

    for copy in scalars + whole:
        copy.wait()
    chosen = lax.broadcasted_iota(I32, (8, ROWS), 1) == pos[0, me] - me * ROWS
    sub = lax.broadcasted_iota(I32, (8, ROWS), 0)
    first = jnp.where(jnp.logical_and(chosen, sub == 0), 1.0, 0.0).astype(BF16)
    second = jnp.where(jnp.logical_and(chosen, sub == 1), 1.0, 0.0).astype(BF16)
    rowt[...] = nn(first, kin[...]) + nn(second, vin[...])

    @pl.when(mine)
    def _():
        pl.semaphore_wait(barrier, SEQ + SHOTS - 2)

    @pl.when(jnp.logical_not(mine))
    def _():
        pl.semaphore_wait(barrier, SEQ - 1)

    def remote(src, dst, send, recv, to):
        return pltpu.make_async_remote_copy(
            src_ref=src, dst_ref=dst, send_sem=send, recv_sem=recv, device_id=to, device_id_type=MESH
        )

    def partner(j):
        return 2 * ((z - zstep(j // 2) + 8) % 8) + (x + j) % 2

    def send_row(j, _):
        t = partner(j)

        @pl.when(owns(t, sh))
        def _():
            cols = at128(head_of(t, sh))
            remote(rowt.at[:, cols], xin.at[me], r_send, r_recv, (sh, t)).start()

        return 0

    def own_row():
        return pltpu.make_async_copy(rowt.at[:, at128(head)], xin.at[me], in_own.at[4])

    def send_kv(j, _):
        t = partner(j)

        @pl.when(owns(t, sh))
        def _():
            cols = at128(head_of(t, sh))
            remote(k.at[0, :, cols], kx.at[at128(me), :], in_send.at[0], kv_recv.at[0], (sh, t)).start()
            remote(v.at[0, :, cols], vx.at[at128(me), :], in_send.at[1], kv_recv.at[1], (sh, t)).start()

        return 0

    def send_qg(j, _):
        t = partner(j)
        i = j // 2

        @pl.when(owns(t, sh))
        def _():
            cols = at128(head_of(t, sh))
            slot = at128(2 * i + x)
            remote(q.at[0, :, cols], qx.at[slot, :], in_send.at[2], q_recv.at[i], (sh, t)).start()
            remote(g.at[0, :, cols], gx.at[slot, :], in_send.at[3], g_recv.at[i], (sh, t)).start()

        return 0

    def own_in(n):
        cols = at128(head)
        src = (k, v, q, g)[n].at[0, :, cols]
        dst = (kx, vx, qx, gx)[n].at[at128(me if n < 2 else x), :]
        return pltpu.make_async_copy(src, dst, in_own.at[n])

    def own_out(n):
        cols = at128(head)
        src = (ox, dqx, dkx, dvx)[n].at[at128(x if n < 2 else me), :]
        dst = (o, dq, lk, lv)[n].at[0, :, cols]
        return pltpu.make_async_copy(src, dst, out_own.at[n])

    def own_c():
        return pltpu.make_async_copy(xc.at[me], xl.at[head], out_own.at[4])

    @pl.when(mine)
    def _():
        for n in range(4):
            own_in(n).start()
        own_row().start()

    lax.fori_loop(1, SEQ, send_row, 0)
    lax.fori_loop(1, EARLY, send_kv, 0)

    @pl.when(mine)
    def _():
        remote(xin.at[pl.ds(0, SEQ - 1)], xin.at[pl.ds(0, SEQ - 1)], r_send, r_recv, (sh, me)).wait_recv()
        own_row().wait()
        dst = pl.ds(pl.multiple_of(OWN + sh * SEQ, SEQ), SEQ)
        for n, buf in enumerate((kx, vx)):
            rows = xin[:, n, :].astype(BF16)
            xs[n] = rows
            buf[dst, :] = rows

        def send_x(j, _):
            to = sibling(j)
            remote(xs.at[0], kx.at[dst, :], x_send.at[0], x_recv.at[0], to).start()
            remote(xs.at[1], vx.at[dst, :], x_send.at[1], x_recv.at[1], to).start()
            return 0

        lax.fori_loop(1, SHOTS, send_x, 0)

    lax.fori_loop(EARLY, SEQ, send_kv, 0)
    lax.fori_loop(1, SEQ, send_qg, 0)

    @pl.when(mine)
    def _():
        length = lens[sh]
        here = (sh, me)
        row = lax.broadcasted_iota(I32, (ROWS, D), 0)
        lane = lax.broadcasted_iota(I32, (ROWS, D), 1)
        for b in range(SEQ):
            alive = jnp.logical_or(row + b * ROWS < length, row + b * ROWS == pos[0, b])
            dead = jnp.logical_and(jnp.logical_not(alive), lane == 0)
            kb[b * ROWS : (b + 1) * ROWS, :] = jnp.where(dead, MASKED, 0.0).astype(BF16)
        for b in range(CROSS // ROWS):
            dead = jnp.logical_and((row + b * ROWS) // SEQ == sh, lane == 0)
            kb[OWN + b * ROWS : OWN + (b + 1) * ROWS, :] = jnp.where(dead, MASKED, 0.0).astype(BF16)
        vt[D : D + 16, :] = jnp.ones((16, KEYS), BF16)
        for n, buf in enumerate((kx, vx)):
            part = buf.at[pl.ds(0, OWN - ROWS), :]
            remote(part, part, in_send.at[n], kv_recv.at[n], here).wait_recv()
            own_in(n).wait()

        def turn(c, _):
            kt[:, at256(c)] = kx[at256(c), :].T
            vt[0:D, at256(c)] = vx[at256(c), :].T
            return 0

        lax.fori_loop(0, OWN // 256, turn, 0)
        for n, buf in enumerate((kx, vx)):
            part = buf.at[pl.ds(OWN, CROSS - SEQ), :]
            remote(part, part, x_send.at[n], x_recv.at[n], here).wait()
        lax.fori_loop(OWN // 256, KEYS // 256, turn, 0)

        def step(i, _):
            for n, (buf, sem) in enumerate(((qx, q_recv), (gx, g_recv))):

                @pl.when(i == 0)
                def _(n=n, buf=buf, sem=sem):
                    part = buf.at[at128(1 - x), :]
                    remote(part, part, in_send.at[2 + n], sem.at[i], here).wait_recv()
                    own_in(2 + n).wait()

                @pl.when(i > 0)
                def _(n=n, buf=buf, sem=sem):
                    part = buf.at[at256(i), :]
                    remote(part, part, in_send.at[2 + n], sem.at[i], here).wait_recv()

            attend(i, kx, vx, kb, qx, gx, kt, vt, logit, prob, dlog, gn, ox, dqx)
            cols = at128(head)
            for d in range(2):
                xt = (x + d) % 2
                to = (sh, 2 * ((z + zstep(i) + 8) % 8) + xt)
                slot = at128(2 * i + xt)

                def start(slot=slot, to=to):
                    remote(ox.at[slot, :], o.at[0, :, cols], out_send.at[0], out_recv.at[0], to).start()
                    remote(dqx.at[slot, :], dq.at[0, :, cols], out_send.at[1], out_recv.at[1], to).start()

                if d == 1:
                    start()
                else:
                    pl.when(i > 0)(start)

                    @pl.when(i == 0)
                    def _():
                        own_out(0).start()
                        own_out(1).start()

            return 0

        lax.fori_loop(0, SEQ // 2, step, 0)

        cross = pl.ds(OWN, CROSS)
        xg[:, 0:SEQ, :] = (nn(dlog[cross, :], qx[...]) * SCALE).reshape(SHOTS, SEQ, D)
        xg[:, SEQ : 2 * SEQ, :] = nn(prob[cross, :], gn[...]).reshape(SHOTS, SEQ, D)
        xr[pl.ds(sh, 1)] = jnp.zeros((1, 2 * SEQ, D), F32)

        def send_g(j, _):
            s = (sh + j) % SHOTS
            remote(xg.at[s], xr.at[sh], x_send.at[2], x_recv.at[2], sibling(j)).start()
            return 0

        lax.fori_loop(1, SHOTS, send_g, 0)

        def send_c(j, _):
            t = (me + j) % SEQ
            remote(xc.at[t], xl.at[head], c_send, c_recv, (sh, t)).start()
            return 0

        def close():
            part = xr.at[pl.ds(0, SHOTS - 1)]
            remote(part, part, x_send.at[2], x_recv.at[2], here).wait()
            total = jnp.sum(xr[...], axis=0)
            xc[...] = jnp.zeros_like(xc)
            for b in range(SEQ):
                xc[b, 0:1, :] = total[b : b + 1, :]
                xc[b, 1:2, :] = total[SEQ + b : SEQ + b + 1, :]
            own_c().start()
            lax.fori_loop(1, SEQ, send_c, 0)

        def finish(i, _):
            pl.when(i == CLOSE)(close)
            zt = (z + zstep(i) + 8) % 8
            rows = at256(zt)
            cols = at128(head)
            dkx[rows, :] = (nn(dlog[rows, :], qx[...]) * SCALE).astype(BF16)
            dvx[rows, :] = nn(prob[rows, :], gn[...]).astype(BF16)
            for d in range(2):
                t = 2 * zt + (x + d) % 2

                def start(t=t):
                    remote(dkx.at[at128(t), :], lk.at[0, :, cols], out_send.at[2], out_recv.at[2], (sh, t)).start()
                    remote(dvx.at[at128(t), :], lv.at[0, :, cols], out_send.at[3], out_recv.at[3], (sh, t)).start()

                if d == 1:
                    start()
                else:
                    pl.when(i > 0)(start)

                    @pl.when(i == 0)
                    def _():
                        own_out(2).start()
                        own_out(3).start()

            return 0

        lax.fori_loop(0, SEQ // 2, finish, 0)

        for n, buf in enumerate((ox, dqx, dkx, dvx)):
            part = buf.at[pl.ds(0, OWN - ROWS), :]
            remote(part, part, out_send.at[n], out_recv.at[n], here).wait_send()
            own_out(n).wait()
        own_c().wait()
        part = xc.at[pl.ds(0, SEQ - 1)]
        remote(part, part, c_send, c_recv, here).wait_send()

    def settle(count):
        here = (sh, me)
        part = xl.at[pl.ds(0, count)]
        remote(part, part, c_send, c_recv, here).wait_recv()
        for n, buf in enumerate((o, dq, lk, lv)):
            part = buf.at[0, :, pl.ds(0, count * D)]
            remote(part, part, out_send.at[n], out_recv.at[n], here).wait_recv()
        part = rowt.at[:, pl.ds(0, count * D)]
        remote(part, part, r_send, r_recv, here).wait_send()
        for n, buf in enumerate((k, v, q, g)):
            part = buf.at[0, :, pl.ds(0, count * D)]
            remote(part, part, in_send.at[n], out_recv.at[n], here).wait_send()

    @pl.when(mine)
    def _():
        settle(HEADS - 1)

    @pl.when(jnp.logical_not(mine))
    def _():
        settle(HEADS)


def hand_over(pos_hbm, o, dq, lk, lv, xl_hbm, o_out, dq_out, dk_out, dv_out, pos, xl, bufs, come, go):
    small = [
        pltpu.make_async_copy(pos_hbm, pos, come.at[4]),
        pltpu.make_async_copy(xl_hbm, xl, come.at[5]),
    ]
    into = [pltpu.make_async_copy(ref, bufs.at[n], come.at[n]) for n, ref in enumerate((lk, lv, o, dq))]
    out = [pltpu.make_async_copy(bufs.at[n], ref, go.at[n]) for n, ref in enumerate((dk_out, dv_out, o_out, dq_out))]
    for copy in small + into:
        copy.start()
    for copy in small:
        copy.wait()
    me = lax.axis_index("seq")
    there = lax.broadcasted_iota(I32, (ROWS, D), 0) == pos[0, me] - me * ROWS
    for n in range(4):
        into[n].wait()
        if n < 2:
            for h in range(HEADS):
                cols = slice(h * D, (h + 1) * D)
                add = jnp.where(there, xl[h][n : n + 1, :], 0.0)
                bufs[n, 0, :, cols] = (bufs[n, 0, :, cols].astype(F32) + add).astype(BF16)
        out[n].start()
    for copy in out:
        copy.wait()


def body(query_rows, key_rows, value_rows, out_grad, shot_lengths, global_positions):
    hbm = pl.BlockSpec(memory_space=pltpu.HBM)
    shape = jax.ShapeDtypeStruct(query_rows.shape, BF16)
    dma = pltpu.SemaphoreType.DMA
    results = pl.pallas_call(
        kernel,
        out_shape=(shape,) * 4 + (jax.ShapeDtypeStruct((HEADS, 8, D), F32),),
        in_specs=[hbm] * 6,
        out_specs=(hbm,) * 5,
        scratch_shapes=[
            pltpu.SMEM((SHOTS,), I32),
            pltpu.SMEM((1, SEQ), I32),
            pltpu.VMEM((KEYS, D), BF16),
            pltpu.VMEM((KEYS, D), BF16),
            pltpu.VMEM((KEYS, D), BF16),
            pltpu.VMEM((OWN, D), BF16),
            pltpu.VMEM((OWN, D), BF16),
            pltpu.VMEM((D, KEYS), BF16),
            pltpu.VMEM((D + 16, KEYS), BF16),
            pltpu.VMEM((KEYS, QB), F32),
            pltpu.VMEM((KEYS, OWN), BF16),
            pltpu.VMEM((KEYS, OWN), BF16),
            pltpu.VMEM((OWN, D), BF16),
            pltpu.VMEM((OWN, D), BF16),
            pltpu.VMEM((OWN, D), BF16),
            pltpu.VMEM((OWN, D), BF16),
            pltpu.VMEM((OWN, D), BF16),
            pltpu.VMEM((ROWS, HEADS * D), BF16),
            pltpu.VMEM((ROWS, HEADS * D), BF16),
            pltpu.VMEM((8, HEADS * D), F32),
            pltpu.VMEM((SEQ, 8, D), F32),
            pltpu.VMEM((2, SEQ, D), BF16),
            pltpu.VMEM((SHOTS, 2 * SEQ, D), F32),
            pltpu.VMEM((SHOTS, 2 * SEQ, D), F32),
            pltpu.VMEM((SEQ, 8, D), F32),
            dma((4,)),
            dma((2,)),
            dma((SEQ // 2,)),
            dma((SEQ // 2,)),
            dma((5,)),
            dma((3,)),
            dma((3,)),
            dma((4,)),
            dma((4,)),
            dma((5,)),
            dma,
            dma,
            dma((4,)),
            dma,
            dma,
        ],
        compiler_params=pltpu.CompilerParams(
            collective_id=0, has_side_effects=True, vmem_limit_bytes=63 << 20
        ),
    )(shot_lengths, global_positions, query_rows, key_rows, value_rows, out_grad)
    return pl.pallas_call(
        hand_over,
        out_shape=(shape,) * 4,
        in_specs=[hbm] * 6,
        out_specs=(hbm,) * 4,
        scratch_shapes=[
            pltpu.SMEM((1, SEQ), I32),
            pltpu.VMEM((HEADS, 8, D), F32),
            pltpu.VMEM((4, 1, ROWS, HEADS * D), BF16),
            dma((6,)),
            dma((4,)),
        ],
        compiler_params=pltpu.CompilerParams(vmem_limit_bytes=63 << 20),
    )(global_positions, *results)


def solution(mesh):
    rows = P("shot", "seq", None)
    return jax.shard_map(
        body,
        mesh=mesh,
        in_specs=(rows, rows, rows, rows, P(), P("shot", None)),
        out_specs=(rows,) * 4,
        check_vma=False,
    )
```

time: 118 us -> 102 us (0.86)
  local copies, waits for them, and re-layouts: 8.27 us -> 0 us
  Pallas kernels: 109 us -> 101 us
    unnamed x16 -> x0, local copies, waits for them, and re-layouts: 8.27 us -> none
    pallas_call x1 -> x2, Pallas kernels: 109 us -> 101 us  [the longest x1 99 us: body(): pl.pallas_call(kernel, out_shape=(shape,) * 4 + (jax.ShapeDtypeStruct((HE...]
where the time goes in v2:
time: 102 us
  Pallas kernels  101 us (99%)
    pallas_call x1, Pallas kernels, body(): pl.pallas_call(kernel, out_shape=(shape,) * 4 + (jax.ShapeDtypeStruct((HE...  99 us
    pallas_call x1, Pallas kernels, body(): pl.pallas_call(hand_over, out_shape=(shape,) * 4, in_specs=[hbm] * 6, out...  2.35 us

profile of v2, /device:TPU:1, one launch (start us, length us, event | category | flops | bytes accessed | tf_op | source)
XLA Modules:
  0.0 102.0 jit_solution(1473577272595347428)
XLA Ops:
  0.6 99.0 %shard_map.93 = (bf16[1,128,1536]{2,1,0:T(8,128)(2,1)}, bf16[1,128,1536]{2,1,0:T(8,128)(2,1)}, bf16[1,128,1536]{2,1,0:T(8,128)(2,1)}, bf16[1,128,1536]{2,1,0:T(8,128)(2,1)}, f32[12,8,128]{2,1,0:T(8,128)}) custom-call(s32[16]{0:T(128)} %lens_hbm.1, s32[1,16]{1,0:T(1,128)} %pos_hbm.3, bf16[1,128,1536]{2,1,0:T(8,128)(2,1)} %q.1, bf16[1,128,1536]{2,1,0:T(8,128)(2,1)} %k.1, ...), custom_call_target="tpu_custom_call" | custom-call | tf_op jit(solution)/shard_map/pallas_call | solution.py:445
  99.7 2.4 %shard_map.94 = (bf16[1,128,1536]{2,1,0:T(8,128)(2,1)}, bf16[1,128,1536]{2,1,0:T(8,128)(2,1)}, bf16[1,128,1536]{2,1,0:T(8,128)(2,1)}, bf16[1,128,1536]{2,1,0:T(8,128)(2,1)}) custom-call(s32[1,16]{1,0:T(1,128)} %pos_hbm.3, bf16[1,128,1536]{2,1,0:T(8,128)(2,1)} %get-tuple-element.9.o, bf16[1,128,1536]{2,1,0:T(8,128)(2,1)} %get-tuple-element.10.dq, ...), custom_call_target="tpu_custom_call" | custom-call | tf_op jit(solution)/shard_map/pallas_call | solution.py:496

commit v3 on v2

--- a/solution.py
+++ b/solution.py
@@ -20,9 +20,8 @@
 SCALE = 1.0 / math.sqrt(D)
 LOGIT2 = SCALE * math.log2(math.e)
 MASKED = -1e30
-EARLY = 5
 CLOSE = 4
-IDLE = ((0, 2, 5, 7), (8, 10, 13, 15))
+IDLE = ((1, 4, 10, 12), (2, 7, 9, 15))
 
 
 def nt(a, b):
@@ -235,7 +234,7 @@
         own_row().start()
 
     lax.fori_loop(1, SEQ, send_row, 0)
-    lax.fori_loop(1, EARLY, send_kv, 0)
+    lax.fori_loop(1, SEQ, send_kv, 0)
 
     @pl.when(mine)
     def _():
@@ -255,7 +254,6 @@
 
         lax.fori_loop(1, SHOTS, send_x, 0)
 
-    lax.fori_loop(EARLY, SEQ, send_kv, 0)
     lax.fori_loop(1, SEQ, send_qg, 0)
 
     @pl.when(mine)

time: 102 us -> 94.5 us (0.926)
  Pallas kernels: 101 us -> 93.4 us
    pallas_call x1, Pallas kernels: 99 us -> 91 us  [body(): pl.pallas_call(kernel, out_shape=(shape,) * 4 + (jax.ShapeDtypeStruct((HE...]
where the time goes in v3:
time: 94.5 us; the launch traced here: 94 us
  Pallas kernels  93.4 us (99%)
    pallas_call x1, Pallas kernels, body(): pl.pallas_call(kernel, out_shape=(shape,) * 4 + (jax.ShapeDtypeStruct((HE...  91 us
    pallas_call x1, Pallas kernels, body(): pl.pallas_call(hand_over, out_shape=(shape,) * 4, in_specs=[hbm] * 6, out...  2.35 us

profile of v3, /device:TPU:1, one launch (start us, length us, event | category | flops | bytes accessed | tf_op | source)
XLA Modules:
  0.0 94.0 jit_solution(10829761390608866576)
XLA Ops:
  0.6 91.0 %shard_map.93 = (bf16[1,128,1536]{2,1,0:T(8,128)(2,1)}, bf16[1,128,1536]{2,1,0:T(8,128)(2,1)}, bf16[1,128,1536]{2,1,0:T(8,128)(2,1)}, bf16[1,128,1536]{2,1,0:T(8,128)(2,1)}, f32[12,8,128]{2,1,0:T(8,128)}) custom-call(s32[16]{0:T(128)} %lens_hbm.1, s32[1,16]{1,0:T(1,128)} %pos_hbm.3, bf16[1,128,1536]{2,1,0:T(8,128)(2,1)} %q.1, bf16[1,128,1536]{2,1,0:T(8,128)(2,1)} %k.1, ...), custom_call_target="tpu_custom_call" | custom-call | tf_op jit(solution)/shard_map/pallas_call | solution.py:443
  91.7 2.4 %shard_map.94 = (bf16[1,128,1536]{2,1,0:T(8,128)(2,1)}, bf16[1,128,1536]{2,1,0:T(8,128)(2,1)}, bf16[1,128,1536]{2,1,0:T(8,128)(2,1)}, bf16[1,128,1536]{2,1,0:T(8,128)(2,1)}) custom-call(s32[1,16]{1,0:T(1,128)} %pos_hbm.3, bf16[1,128,1536]{2,1,0:T(8,128)(2,1)} %get-tuple-element.9.o, bf16[1,128,1536]{2,1,0:T(8,128)(2,1)} %get-tuple-element.10.dq, ...), custom_call_target="tpu_custom_call" | custom-call | tf_op jit(solution)/shard_map/pallas_call | solution.py:494

commit v4 on v3

--- a/solution.py
+++ b/solution.py
@@ -21,7 +21,7 @@
 LOGIT2 = SCALE * math.log2(math.e)
 MASKED = -1e30
 CLOSE = 4
-IDLE = ((1, 4, 10, 12), (2, 7, 9, 15))
+IDLE = ((1, 4, 11, 14), (3, 6, 9, 12))
 
 
 def nt(a, b):

time: 94.5 us -> 93.1 us (0.985)
  Pallas kernels: 93.4 us -> 92.3 us
    pallas_call x1, Pallas kernels: 91 us -> 90 us  [body(): pl.pallas_call(kernel, out_shape=(shape,) * 4 + (jax.ShapeDtypeStruct((HE...]
where the time goes in v4:
time: 93.1 us; the launch traced here: 93 us
  Pallas kernels  92.3 us (99%)
    pallas_call x1, Pallas kernels, body(): pl.pallas_call(kernel, out_shape=(shape,) * 4 + (jax.ShapeDtypeStruct((HE...  90 us
    pallas_call x1, Pallas kernels, body(): pl.pallas_call(hand_over, out_shape=(shape,) * 4, in_specs=[hbm] * 6, out...  2.35 us

profile of v4, /device:TPU:1, one launch (start us, length us, event | category | flops | bytes accessed | tf_op | source)
XLA Modules:
  0.0 93.0 jit_solution(11716989079881634432)
XLA Ops:
  0.6 90.0 %shard_map.93 = (bf16[1,128,1536]{2,1,0:T(8,128)(2,1)}, bf16[1,128,1536]{2,1,0:T(8,128)(2,1)}, bf16[1,128,1536]{2,1,0:T(8,128)(2,1)}, bf16[1,128,1536]{2,1,0:T(8,128)(2,1)}, f32[12,8,128]{2,1,0:T(8,128)}) custom-call(s32[16]{0:T(128)} %lens_hbm.1, s32[1,16]{1,0:T(1,128)} %pos_hbm.3, bf16[1,128,1536]{2,1,0:T(8,128)(2,1)} %q.1, bf16[1,128,1536]{2,1,0:T(8,128)(2,1)} %k.1, ...), custom_call_target="tpu_custom_call" | custom-call | tf_op jit(solution)/shard_map/pallas_call | solution.py:443
  90.6 2.4 %shard_map.94 = (bf16[1,128,1536]{2,1,0:T(8,128)(2,1)}, bf16[1,128,1536]{2,1,0:T(8,128)(2,1)}, bf16[1,128,1536]{2,1,0:T(8,128)(2,1)}, bf16[1,128,1536]{2,1,0:T(8,128)(2,1)}) custom-call(s32[1,16]{1,0:T(1,128)} %pos_hbm.3, bf16[1,128,1536]{2,1,0:T(8,128)(2,1)} %get-tuple-element.9.o, bf16[1,128,1536]{2,1,0:T(8,128)(2,1)} %get-tuple-element.10.dq, ...), custom_call_target="tpu_custom_call" | custom-call | tf_op jit(solution)/shard_map/pallas_call | solution.py:494

commit v5 on v4

--- a/solution.py
+++ b/solution.py
@@ -64,7 +64,7 @@
     return pl.ds(pl.multiple_of(i * 256, 256), 256)
 
 
-def attend(i, kx, vx, kb, qx, gx, kt, vt, logit, prob, dlog, gn, ox, dqx):
+def attend(i, kx, vx, kb, qx, gx, kt, vt, logit, prob, dlog, gn, ox, dqx, send):
     rows = at256(i)
     q = qx[rows, :]
     g = gx[rows, :]
@@ -89,6 +89,7 @@
     inv = 1.0 / both[:, 128:]
     att = (both[:, :128] * inv).astype(BF16)
     ox[rows, :] = att
+    send(0)
     gf = g.astype(F32)
     delta = jnp.sum(gf * att.astype(F32), axis=1, keepdims=True) * inv
     gs = (gf * inv).astype(BF16)
@@ -108,6 +109,7 @@
         part = nn(kt[:, ks], ds)
         acc = part if acc is None else acc + part
     dqx[rows, :] = (acc * SCALE).T.astype(BF16)
+    send(1)
 
 
 def kernel(
@@ -300,27 +302,28 @@
                     part = buf.at[at256(i), :]
                     remote(part, part, in_send.at[2 + n], sem.at[i], here).wait_recv()
 
-            attend(i, kx, vx, kb, qx, gx, kt, vt, logit, prob, dlog, gn, ox, dqx)
             cols = at128(head)
-            for d in range(2):
-                xt = (x + d) % 2
-                to = (sh, 2 * ((z + zstep(i) + 8) % 8) + xt)
-                slot = at128(2 * i + xt)
-
-                def start(slot=slot, to=to):
-                    remote(ox.at[slot, :], o.at[0, :, cols], out_send.at[0], out_recv.at[0], to).start()
-                    remote(dqx.at[slot, :], dq.at[0, :, cols], out_send.at[1], out_recv.at[1], to).start()
-
-                if d == 1:
-                    start()
-                else:
-                    pl.when(i > 0)(start)
-
-                    @pl.when(i == 0)
-                    def _():
-                        own_out(0).start()
-                        own_out(1).start()
-
+
+            def send(n):
+                src, dst = ((ox, o), (dqx, dq))[n]
+                for d in range(2):
+                    xt = (x + d) % 2
+                    to = (sh, 2 * ((z + zstep(i) + 8) % 8) + xt)
+                    slot = at128(2 * i + xt)
+
+                    def start(slot=slot, to=to):
+                        remote(src.at[slot, :], dst.at[0, :, cols], out_send.at[n], out_recv.at[n], to).start()
+
+                    if d == 1:
+                        start()
+                    else:
+                        pl.when(i > 0)(start)
+
+                        @pl.when(i == 0)
+                        def _():
+                            own_out(n).start()
+
+            attend(i, kx, vx, kb, qx, gx, kt, vt, logit, prob, dlog, gn, ox, dqx, send)
             return 0
 
         lax.fori_loop(0, SEQ // 2, step, 0)

time: 93.1 us -> 93.3 us (level)
  no operation moved by 1% of the time
where the time goes in v5:
time: 93.3 us; the launch traced here: 93.1 us
  Pallas kernels  92.5 us (99%)
    pallas_call x1, Pallas kernels, body(): pl.pallas_call(kernel, out_shape=(shape,) * 4 + (jax.ShapeDtypeStruct((HE...  90.1 us
    pallas_call x1, Pallas kernels, body(): pl.pallas_call(hand_over, out_shape=(shape,) * 4, in_specs=[hbm] * 6, out...  2.35 us

profile of v5, /device:TPU:1, one launch (start us, length us, event | category | flops | bytes accessed | tf_op | source)
XLA Modules:
  0.0 93.1 jit_solution(9757554899553257521)
XLA Ops:
  0.6 90.1 %shard_map.93 = (bf16[1,128,1536]{2,1,0:T(8,128)(2,1)}, bf16[1,128,1536]{2,1,0:T(8,128)(2,1)}, bf16[1,128,1536]{2,1,0:T(8,128)(2,1)}, bf16[1,128,1536]{2,1,0:T(8,128)(2,1)}, f32[12,8,128]{2,1,0:T(8,128)}) custom-call(s32[16]{0:T(128)} %lens_hbm.1, s32[1,16]{1,0:T(1,128)} %pos_hbm.3, bf16[1,128,1536]{2,1,0:T(8,128)(2,1)} %q.1, bf16[1,128,1536]{2,1,0:T(8,128)(2,1)} %k.1, ...), custom_call_target="tpu_custom_call" | custom-call | tf_op jit(solution)/shard_map/pallas_call | solution.py:446
  90.8 2.4 %shard_map.94 = (bf16[1,128,1536]{2,1,0:T(8,128)(2,1)}, bf16[1,128,1536]{2,1,0:T(8,128)(2,1)}, bf16[1,128,1536]{2,1,0:T(8,128)(2,1)}, bf16[1,128,1536]{2,1,0:T(8,128)(2,1)}) custom-call(s32[1,16]{1,0:T(1,128)} %pos_hbm.3, bf16[1,128,1536]{2,1,0:T(8,128)(2,1)} %get-tuple-element.9.o, bf16[1,128,1536]{2,1,0:T(8,128)(2,1)} %get-tuple-element.10.dq, ...), custom_call_target="tpu_custom_call" | custom-call | tf_op jit(solution)/shard_map/pallas_call | solution.py:497
